TPU v7x, 32 devices: a whole 2x2x4 slice. The times are simulated.
32 devices in a mesh: rep: 2 (over y), seq: 4 (over x, core), head: 4 (over z).
Axes of the slice: x: 2, y: 2, z: 4, core: 2. Of those that a mesh axis runs over, the one named last changes fastest.
Arguments:
- queries: bfloat16 [2048, 4096], P(('rep', 'seq', 'head')), parts along dimension 0, may hold values from -6 to 6
- key_rows: bfloat16 [2048, 4096], P(('rep', 'seq', 'head')), parts along dimension 0, may hold values from -6 to 6
- value_rows: bfloat16 [2048, 4096], P(('rep', 'seq', 'head')), parts along dimension 0, may hold values from -6 to 6
- out_grad: bfloat16 [2048, 4096], P(('rep', 'seq', 'head')), parts along dimension 0, may hold values from -6 to 6
Outputs:
- attended: bfloat16 [2048, 4096], P(('rep', 'seq', 'head')), parts along dimension 0
- query_grad: bfloat16 [2048, 4096], P(('rep', 'seq', 'head')), parts along dimension 0
- key_grad: bfloat16 [2048, 4096], P(('rep', 'seq', 'head')), parts along dimension 0
- value_grad: bfloat16 [2048, 4096], P(('rep', 'seq', 'head')), parts along dimension 0
There are 2 independent parts, one for each index of `rep`. A program takes and returns all parts, laid end to end along the dimension named above; each array names one. Nothing has to cross between parts.
All inputs are finite; a program needn't handle non-finite values.
Results may differ from a plain program's by a relative error of at most 0.0049.
Values may be sent and summed in bfloat16 or wider, within the bound.
A program may use at most 64 MiB of HBM per device.

v0:
```python
import jax
import jax.numpy as jnp
from jax import lax
from jax.sharding import PartitionSpec as P

DH = 128
BLK_MAX = 512


def shards(queries, key_rows, value_rows, out_grad):
    f32 = jnp.float32
    bf16 = jnp.bfloat16
    head_count = lax.axis_size("head")
    tok_count = queries.shape[0]
    local_heads = queries.shape[1] // (head_count * DH)
    seq_rows = tok_count * head_count
    block = min(BLK_MAX, seq_rows)
    block_count = seq_rows // block
    factor = float(DH * seq_rows * lax.axis_size("seq")) ** (-0.5)

    def to_heads(matrix):
        return matrix.reshape(tok_count, head_count, local_heads, DH)

    def per_head(parts):
        heads_here = parts[0].shape[2]
        query_blocks, key_blocks, value_blocks, grad_blocks = (
            item.reshape(block_count, block, heads_here, DH) for item in parts
        )
        kv_state = jnp.einsum(
            "bthd,bthe->bhde", key_blocks, value_blocks, preferred_element_type=f32
        )
        grad_state = jnp.einsum(
            "bthd,bthe->bhde", query_blocks, grad_blocks, preferred_element_type=f32
        )
        empty_state = jnp.zeros((1, heads_here, DH, DH), f32)
        local_prefix = jnp.concatenate([empty_state, jnp.cumsum(kv_state, 0)[:-1]], 0)
        tail_sums = jnp.cumsum(grad_state[::-1], 0)[::-1]
        local_suffix = jnp.concatenate([tail_sums[1:], empty_state], 0)
        kv_total = jnp.sum(kv_state, 0)
        grad_total = jnp.sum(grad_state, 0)
        my_index = lax.axis_index("seq")
        pieces = (
            lax.all_gather(kv_total[None], "seq", axis=0, tiled=True),
            lax.all_gather(grad_total[None], "seq", axis=0, tiled=True),
        )
        count = pieces[0].shape[0]
        index = jnp.arange(count, dtype=jnp.int32)
        below_me = (index < my_index).astype(f32)[:, None, None, None]
        above_me = (index > my_index).astype(f32)[:, None, None, None]
        span_prefix = jnp.sum(pieces[0] * below_me, 0)
        span_suffix = jnp.sum(pieces[1] * above_me, 0)
        prefix = (local_prefix + span_prefix[None]).astype(bf16)
        suffix = (local_suffix + span_suffix[None]).astype(bf16)
        causal = (jnp.arange(block)[:, None] >= jnp.arange(block)[None, :])[None, None]
        scores = jnp.einsum("bthd,bshd->bhts", query_blocks, key_blocks, preferred_element_type=f32)
        scores = jnp.where(causal, scores * factor, 0.0).astype(bf16)
        attended = jnp.einsum("bhts,bshd->bthd", scores, value_blocks, preferred_element_type=f32)
        attended = attended + factor * jnp.einsum(
            "bthd,bhde->bthe", query_blocks, prefix, preferred_element_type=f32
        )
        dscores = jnp.einsum(
            "bthe,bshe->bhts", grad_blocks, value_blocks, preferred_element_type=f32
        )
        dscores = jnp.where(causal, dscores * factor, 0.0).astype(bf16)
        query_grad = jnp.einsum("bhts,bshd->bthd", dscores, key_blocks, preferred_element_type=f32)
        query_grad = query_grad + factor * jnp.einsum(
            "bthe,bhde->bthd", grad_blocks, prefix, preferred_element_type=f32
        )
        key_grad = jnp.einsum("bhts,bthd->bshd", dscores, query_blocks, preferred_element_type=f32)
        key_grad = key_grad + factor * jnp.einsum(
            "bshe,bhde->bshd", value_blocks, suffix, preferred_element_type=f32
        )
        value_grad = jnp.einsum("bhts,bthe->bshe", scores, grad_blocks, preferred_element_type=f32)
        value_grad = value_grad + factor * jnp.einsum(
            "bshd,bhde->bshe", key_blocks, suffix, preferred_element_type=f32
        )
        results = tuple(
            (
                item.astype(bf16).reshape(seq_rows, 1, heads_here, DH)
                for item in (attended, query_grad, key_grad, value_grad)
            )
        )
        return (
            lax.all_to_all(results[0], "head", split_axis=0, concat_axis=1, tiled=True),
            lax.all_to_all(results[1], "head", split_axis=0, concat_axis=1, tiled=True),
            lax.all_to_all(results[2], "head", split_axis=0, concat_axis=1, tiled=True),
            lax.all_to_all(results[3], "head", split_axis=0, concat_axis=1, tiled=True),
        )

    outputs = per_head(
        (
            lax.all_to_all(to_heads(queries), "head", split_axis=1, concat_axis=0, tiled=True),
            lax.all_to_all(to_heads(key_rows), "head", split_axis=1, concat_axis=0, tiled=True),
            lax.all_to_all(to_heads(value_rows), "head", split_axis=1, concat_axis=0, tiled=True),
            lax.all_to_all(to_heads(out_grad), "head", split_axis=1, concat_axis=0, tiled=True),
        )
    )
    return tuple((item.reshape(tok_count, queries.shape[1]) for item in outputs))


def solution(mesh):
    placed = (
        P(("rep", "seq", "head"), None),
        P(("rep", "seq", "head"), None),
        P(("rep", "seq", "head"), None),
        P(("rep", "seq", "head"), None),
    )
    return jax.shard_map(
        shards,
        mesh=mesh,
        in_specs=placed,
        out_specs=(
            P(("rep", "seq", "head"), None),
            P(("rep", "seq", "head"), None),
            P(("rep", "seq", "head"), None),
            P(("rep", "seq", "head"), None),
        ),
        check_vma=False,
    )
```

profile of v0, /device:TPU:2, one launch (start us, length us, event | category | flops | bytes accessed | tf_op | source)
XLA Modules:
  0.0 171.7 jit_solution(1147366358603336593)
XLA Ops:
  7.2 1.2 copy.85
  9.4 4.9 %all-to-all-start.1 = ((bf16[64,4,8,128]{3,0,2,1:T(8,128)(2,1)}), bf16[64,4,8,128]{3,0,2,1:T(8,128)(2,1)S(1)}, u32[]{:S(2)}, u32[]{:S(2)}) async-start(bf16[64,4,8,128]{3,0,2,1:T(8,128)(2,1)} %copy.50), calls=%async_computation.1 | async-start | bytes 1048576 | tf_op jit(solution)/shard_map/all_to_all | solution.py:93
  15.3 13.4 %all-to-all-done.1 = bf16[64,4,8,128]{3,0,2,1:T(8,128)(2,1)S(1)} async-done(((bf16[64,4,8,128]{3,0,2,1:T(8,128)(2,1)}), bf16[64,4,8,128]{3,0,2,1:T(8,128)(2,1)S(1)}, u32[]{:S(2)}, u32[]{:S(2)}) %all-to-all-start.1) | async-done | bytes 524320 | tf_op jit(solution)/shard_map/all_to_all | solution.py:93
  28.7 3.5 %all-to-all-start.2 = ((bf16[64,4,8,128]{3,0,2,1:T(8,128)(2,1)}), bf16[64,4,8,128]{3,0,2,1:T(8,128)(2,1)S(1)}, u32[]{:S(2)}, u32[]{:S(2)}) async-start(bf16[64,4,8,128]{3,0,2,1:T(8,128)(2,1)} %copy.52), calls=%async_computation.2 | async-start | bytes 1048576 | tf_op jit(solution)/shard_map/all_to_all | solution.py:94
  32.3 13.9 %all-to-all-done.2 = bf16[64,4,8,128]{3,0,2,1:T(8,128)(2,1)S(1)} async-done(((bf16[64,4,8,128]{3,0,2,1:T(8,128)(2,1)}), bf16[64,4,8,128]{3,0,2,1:T(8,128)(2,1)S(1)}, u32[]{:S(2)}, u32[]{:S(2)}) %all-to-all-start.2) | async-done | bytes 524320 | tf_op jit(solution)/shard_map/all_to_all | solution.py:94
  46.2 1.1 fusion.16
  48.5 3.5 %all-to-all-start = ((bf16[64,4,8,128]{3,0,2,1:T(8,128)(2,1)}), bf16[64,4,8,128]{3,0,2,1:T(8,128)(2,1)S(1)}, u32[]{:S(2)}, u32[]{:S(2)}) async-start(bf16[64,4,8,128]{3,0,2,1:T(8,128)(2,1)} %copy.48), calls=%async_computation | async-start | bytes 1048576 | tf_op jit(solution)/shard_map/all_to_all | solution.py:92
  53.1 12.8 %all-to-all-done = bf16[64,4,8,128]{3,0,2,1:T(8,128)(2,1)S(1)} async-done(((bf16[64,4,8,128]{3,0,2,1:T(8,128)(2,1)}), bf16[64,4,8,128]{3,0,2,1:T(8,128)(2,1)S(1)}, u32[]{:S(2)}, u32[]{:S(2)}) %all-to-all-start) | async-done | bytes 524320 | tf_op jit(solution)/shard_map/all_to_all | solution.py:92
  65.9 3.5 %all-to-all-start.4 = ((bf16[64,4,8,128]{3,0,2,1:T(8,128)(2,1)}), bf16[64,4,8,128]{3,0,2,1:T(8,128)(2,1)S(1)}, u32[]{:S(2)}, u32[]{:S(2)}) async-start(bf16[64,4,8,128]{3,0,2,1:T(8,128)(2,1)} %copy.59), calls=%async_computation.4 | async-start | bytes 1048576 | tf_op jit(solution)/shard_map/all_to_all | solution.py:95
  69.5 13.9 %all-to-all-done.4 = bf16[64,4,8,128]{3,0,2,1:T(8,128)(2,1)S(1)} async-done(((bf16[64,4,8,128]{3,0,2,1:T(8,128)(2,1)}), bf16[64,4,8,128]{3,0,2,1:T(8,128)(2,1)S(1)}, u32[]{:S(2)}, u32[]{:S(2)}) %all-to-all-start.4) | async-done | bytes 524320 | tf_op jit(solution)/shard_map/all_to_all | solution.py:95
  83.4 1.1 fusion.17
  85.1 1.4 convolution_bitcast_fusion.3
  86.5 1.9 %multiply_reduce_fusion.1 = bf16[8,128,128]{2,1,0:T(8,128)(2,1)S(1)} fusion(f32[4,8,128,128]{3,2,1,0:T(8,128)} %bitcast.130, f32[4]{0:T(128)S(1)} %compare_convert_fusion.1), kind=kLoop, calls=%fused_computation.2 | loop fusion | flops 917504 | bytes 2359312 | tf_op jit(solution)/shard_map/reduce_sum | solution.py:50
  88.7 1.1 copy.57
  89.9 4.2 %all-to-all-start.3 = ((bf16[256,1,8,128]{3,2,1,0:T(8,128)(2,1)}), bf16[256,1,8,128]{3,2,1,0:T(8,128)(2,1)}, u32[]{:S(2)}, u32[]{:S(2)}) async-start(bf16[256,1,8,128]{3,2,1,0:T(8,128)(2,1)} %copy.57), calls=%async_computation.3 | async-start | bytes 1048576 | tf_op jit(solution)/shard_map/all_to_all | solution.py:84
  94.0 1.5 convolution_bitcast_fusion
  95.5 9.7 %all-gather.7.cloned.1.call-done = f32[32,128,128]{2,1,0:T(8,128)} async-done(((f32[8,128,128]{2,1,0:T(8,128)}), f32[32,128,128]{2,1,0:T(8,128)}) %all-gather.7.cloned.1.call-update) | async-done | bytes 2097168 | tf_op jit(solution)/shard_map/all_gather | solution.py:44
  105.2 1.9 %multiply_reduce_fusion = bf16[8,128,128]{2,1,0:T(8,128)(2,1)S(1)} fusion(f32[4,8,128,128]{3,2,1,0:T(8,128)} %bitcast.131, f32[4]{0:T(128)S(1)} %compare_convert_fusion), kind=kLoop, calls=%fused_computation | loop fusion | flops 917504 | bytes 2359312 | tf_op jit(solution)/shard_map/reduce_sum | solution.py:51
  107.8 1.1 copy.72
  108.9 4.8 %all-to-all-start.7 = ((bf16[256,1,8,128]{3,2,1,0:T(8,128)(2,1)}), bf16[256,1,8,128]{3,2,1,0:T(8,128)(2,1)}, u32[]{:S(2)}, u32[]{:S(2)}) async-start(bf16[256,1,8,128]{3,2,1,0:T(8,128)(2,1)} %copy.72), calls=%async_computation.7 | async-start | bytes 1048576 | tf_op jit(solution)/shard_map/all_to_all | solution.py:87
  115.0 1.1 copy.67
  116.2 12.6 %all-to-all-done.7 = bf16[256,1,8,128]{3,2,1,0:T(8,128)(2,1)} async-done(((bf16[256,1,8,128]{3,2,1,0:T(8,128)(2,1)}), bf16[256,1,8,128]{3,2,1,0:T(8,128)(2,1)}, u32[]{:S(2)}, u32[]{:S(2)}) %all-to-all-start.7) | async-done | bytes 524320 | tf_op jit(solution)/shard_map/all_to_all | solution.py:87
  128.8 3.5 %all-to-all-start.6 = ((bf16[256,1,8,128]{3,2,1,0:T(8,128)(2,1)}), bf16[256,1,8,128]{3,2,1,0:T(8,128)(2,1)S(1)}, u32[]{:S(2)}, u32[]{:S(2)}) async-start(bf16[256,1,8,128]{3,2,1,0:T(8,128)(2,1)} %copy.67), calls=%async_computation.6 | async-start | bytes 1048576 | tf_op jit(solution)/shard_map/all_to_all | solution.py:86
  133.0 1.1 copy.62
  134.1 12.1 %all-to-all-done.6 = bf16[256,1,8,128]{3,2,1,0:T(8,128)(2,1)S(1)} async-done(((bf16[256,1,8,128]{3,2,1,0:T(8,128)(2,1)}), bf16[256,1,8,128]{3,2,1,0:T(8,128)(2,1)S(1)}, u32[]{:S(2)}, u32[]{:S(2)}) %all-to-all-start.6) | async-done | bytes 524320 | tf_op jit(solution)/shard_map/all_to_all | solution.py:86
  146.3 3.5 %all-to-all-start.5 = ((bf16[256,1,8,128]{3,2,1,0:T(8,128)(2,1)}), bf16[256,1,8,128]{3,2,1,0:T(8,128)(2,1)S(1)}, u32[]{:S(2)}, u32[]{:S(2)}) async-start(bf16[256,1,8,128]{3,2,1,0:T(8,128)(2,1)} %copy.62), calls=%async_computation.5 | async-start | bytes 1048576 | tf_op jit(solution)/shard_map/all_to_all | solution.py:85
  149.8 1.1 copy.58
  150.9 1.0 reshape.189
  151.9 1.1 copy.73
  153.0 1.0 reshape.197
  154.2 1.0 reshape.195
  155.2 8.5 %all-to-all-done.5 = bf16[256,1,8,128]{3,2,1,0:T(8,128)(2,1)S(1)} async-done(((bf16[256,1,8,128]{3,2,1,0:T(8,128)(2,1)}), bf16[256,1,8,128]{3,2,1,0:T(8,128)(2,1)S(1)}, u32[]{:S(2)}, u32[]{:S(2)}) %all-to-all-start.5) | async-done | bytes 524320 | tf_op jit(solution)/shard_map/all_to_all | solution.py:85
  (45 shorter events, 9.2 us)
Async XLA Ops:
  7.2 7.1 %copy-start.4 = (bf16[64,4096]{1,0:T(8,128)(2,1)S(1)}, bf16[64,4096]{1,0:T(8,128)(2,1)}, u32[]{:S(2)}) copy-start(bf16[64,4096]{1,0:T(8,128)(2,1)} %param.6) | copy-start | bytes 1572868
  9.4 19.4 %all-to-all-start.1 = ((bf16[64,4,8,128]{3,0,2,1:T(8,128)(2,1)}), bf16[64,4,8,128]{3,0,2,1:T(8,128)(2,1)S(1)}, u32[]{:S(2)}, u32[]{:S(2)}) async-start(bf16[64,4,8,128]{3,0,2,1:T(8,128)(2,1)} %copy.50), calls=%async_computation.1 | async-start | bytes 1048576 | tf_op jit(solution)/shard_map/all_to_all | solution.py:93
  28.7 17.4 %all-to-all-start.2 = ((bf16[64,4,8,128]{3,0,2,1:T(8,128)(2,1)}), bf16[64,4,8,128]{3,0,2,1:T(8,128)(2,1)S(1)}, u32[]{:S(2)}, u32[]{:S(2)}) async-start(bf16[64,4,8,128]{3,0,2,1:T(8,128)(2,1)} %copy.52), calls=%async_computation.2 | async-start | bytes 1048576 | tf_op jit(solution)/shard_map/all_to_all | solution.py:94
  32.2 54.3 %all-gather.5.cloned.1.call-start = ((), (), s32[]{:S(2)}) async-start(), calls=%async_computation.8 | async-start | bytes 2621440 | tf_op jit(solution)/shard_map/all_gather | solution.py:43
  32.3 15.1 %copy-start.5 = (bf16[64,4096]{1,0:T(8,128)(2,1)S(1)}, bf16[64,4096]{1,0:T(8,128)(2,1)}, u32[]{:S(2)}) copy-start(bf16[64,4096]{1,0:T(8,128)(2,1)} %param.4) | copy-start | bytes 1572868
  47.4 4.6 %copy-start.6 = (bf16[64,4096]{1,0:T(8,128)(2,1)S(1)}, bf16[64,4096]{1,0:T(8,128)(2,1)}, u32[]{:S(2)}) copy-start(bf16[64,4096]{1,0:T(8,128)(2,1)} %param.7) | copy-start | bytes 1572868
  48.5 17.4 %all-to-all-start = ((bf16[64,4,8,128]{3,0,2,1:T(8,128)(2,1)}), bf16[64,4,8,128]{3,0,2,1:T(8,128)(2,1)S(1)}, u32[]{:S(2)}, u32[]{:S(2)}) async-start(bf16[64,4,8,128]{3,0,2,1:T(8,128)(2,1)} %copy.48), calls=%async_computation | async-start | bytes 1048576 | tf_op jit(solution)/shard_map/all_to_all | solution.py:92
  65.9 17.4 %all-to-all-start.4 = ((bf16[64,4,8,128]{3,0,2,1:T(8,128)(2,1)}), bf16[64,4,8,128]{3,0,2,1:T(8,128)(2,1)S(1)}, u32[]{:S(2)}, u32[]{:S(2)}) async-start(bf16[64,4,8,128]{3,0,2,1:T(8,128)(2,1)} %copy.59), calls=%async_computation.4 | async-start | bytes 1048576 | tf_op jit(solution)/shard_map/all_to_all | solution.py:95
  69.4 35.8 %all-gather.7.cloned.1.call-start = ((), (), s32[]{:S(2)}) async-start(), calls=%async_computation.9 | async-start | bytes 2621440 | tf_op jit(solution)/shard_map/all_gather | solution.py:44
  86.5 1.9 %copy-start.1 = (f32[8,128,256]{1,2,0:T(8,128)S(1)}, f32[8,128,256]{1,2,0:T(8,128)}, u32[]{:S(2)}) copy-start(f32[8,128,256]{1,2,0:T(8,128)} %convolution_bitcast_fusion.3) | copy-start | bytes 3145732
  89.9 19.1 %all-to-all-start.3 = ((bf16[256,1,8,128]{3,2,1,0:T(8,128)(2,1)}), bf16[256,1,8,128]{3,2,1,0:T(8,128)(2,1)}, u32[]{:S(2)}, u32[]{:S(2)}) async-start(bf16[256,1,8,128]{3,2,1,0:T(8,128)(2,1)} %copy.57), calls=%async_computation.3 | async-start | bytes 1048576 | tf_op jit(solution)/shard_map/all_to_all | solution.py:84
  95.5 11.6 %copy-start = (f32[8,128,256]{1,2,0:T(8,128)S(1)}, f32[8,128,256]{1,2,0:T(8,128)}, u32[]{:S(2)}) copy-start(f32[8,128,256]{1,2,0:T(8,128)} %convolution_bitcast_fusion) | copy-start | bytes 3145732
  107.1 0.7 copy-start.2
  108.9 19.8 %all-to-all-start.7 = ((bf16[256,1,8,128]{3,2,1,0:T(8,128)(2,1)}), bf16[256,1,8,128]{3,2,1,0:T(8,128)(2,1)}, u32[]{:S(2)}, u32[]{:S(2)}) async-start(bf16[256,1,8,128]{3,2,1,0:T(8,128)(2,1)} %copy.72), calls=%async_computation.7 | async-start | bytes 1048576 | tf_op jit(solution)/shard_map/all_to_all | solution.py:87
  113.8 0.9 copy-start.3
  128.8 17.5 %all-to-all-start.6 = ((bf16[256,1,8,128]{3,2,1,0:T(8,128)(2,1)}), bf16[256,1,8,128]{3,2,1,0:T(8,128)(2,1)S(1)}, u32[]{:S(2)}, u32[]{:S(2)}) async-start(bf16[256,1,8,128]{3,2,1,0:T(8,128)(2,1)} %copy.67), calls=%async_computation.6 | async-start | bytes 1048576 | tf_op jit(solution)/shard_map/all_to_all | solution.py:86
  146.3 17.4 %all-to-all-start.5 = ((bf16[256,1,8,128]{3,2,1,0:T(8,128)(2,1)}), bf16[256,1,8,128]{3,2,1,0:T(8,128)(2,1)S(1)}, u32[]{:S(2)}, u32[]{:S(2)}) async-start(bf16[256,1,8,128]{3,2,1,0:T(8,128)(2,1)} %copy.62), calls=%async_computation.5 | async-start | bytes 1048576 | tf_op jit(solution)/shard_map/all_to_all | solution.py:85
Sparse Core Ops, SparseCore 0:
  47.5 20.5 all-gather.4
  84.7 20.4 all-gather.6
where the time goes:
time: 175 us; the launch traced here: 172 us
  waiting for transfers between devices  97 us (55%)
  starting transfers between devices  31.3 us (18%)
  local copies, waits for them, and re-layouts  17.1 us (10%)
  between operations  14.3 us (8%)
  matrix products  8.13 us (5%)
  other arithmetic  3.83 us (2%)
    all_to_all x1, waiting for transfers between devices, shards(): lax.all_to_all(to_heads(out_grad), 'head', split_axis=1, concat_axis=0, t...  13.9 us
    all_to_all x1, waiting for transfers between devices, shards(): lax.all_to_all(to_heads(value_rows), 'head', split_axis=1, concat_axis=0,...  13.9 us
    all_to_all x1, waiting for transfers between devices, shards(): lax.all_to_all(to_heads(key_rows), 'head', split_axis=1, concat_axis=0, t...  13.4 us
    all_to_all x1, waiting for transfers between devices, shards(): lax.all_to_all(to_heads(queries), 'head', split_axis=1, concat_axis=0, ti...  12.8 us
    all_to_all x1, waiting for transfers between devices, per_head(): lax.all_to_all(results[3], 'head', split_axis=0, concat_axis=1, tiled=True)  12.6 us
    all_to_all x1, waiting for transfers between devices, per_head(): lax.all_to_all(results[2], 'head', split_axis=0, concat_axis=1, tiled=True)  12.1 us
    all_gather x1, waiting for transfers between devices, per_head(): lax.all_gather(grad_total[None], 'seq', axis=0, tiled=True)  9.71 us
    all_to_all x1, waiting for transfers between devices, per_head(): lax.all_to_all(results[1], 'head', split_axis=0, concat_axis=1, tiled=True)  8.53 us
  transfers between devices with their start and end apart: 10, of which 8 were waited for; matrix products, arithmetic and copies ran while one was open for 14% of the time, Pallas kernels for 0%

commit v1 on v0

v1 whole, which is shorter than its diff:
```python
import functools

import jax
import jax.numpy as jnp
from jax import lax
from jax.experimental import pallas as pl
from jax.experimental.pallas import tpu as pltpu
from jax.sharding import PartitionSpec as P

DH = 128
HEADS_PER_CHUNK = 2
SEQ_LAG = 1
TOK_LAG = 1

F32 = jnp.float32
BF16 = jnp.bfloat16


def dot(a, b, ca, cb):
    return lax.dot_general(a, b, (((ca,), (cb,)), ((), ())), preferred_element_type=F32)


def kernel(
    n_s, n_h, heads, per, factor, zdt,
    q_ref, k_ref, v_ref, g_ref,
    att_ref, dq_ref, dk_ref, dv_ref,
    own_kv, own_gs, s_send, s_recv, t_send, t_recv,
    up_send, up_recv, dn_send, dn_recv,
    s_ss, s_rs, t_ss, t_rs, up_ss, up_rs, dn_ss, dn_rs,
):
    s = lax.axis_index("seq")
    h = lax.axis_index("head")
    chunks = heads // per
    toks = q_ref.shape[0]

    def seq_copy(src, dst, ss, rs, i, to):
        return pltpu.make_async_remote_copy(
            src_ref=src.at[pl.ds(i * per, per)],
            dst_ref=dst.at[pl.ds(i * per, per)],
            send_sem=ss.at[i],
            recv_sem=rs.at[i],
            device_id={"seq": to},
            device_id_type=pl.DeviceIdType.MESH,
        )

    def head_copy(src, dst, ss, rs, i, to):
        return pltpu.make_async_remote_copy(
            src_ref=src.at[i],
            dst_ref=dst.at[i],
            send_sem=ss.at[i],
            recv_sem=rs.at[i],
            device_id={"head": to},
            device_id_type=pl.DeviceIdType.MESH,
        )

    s_next, s_prev = lax.rem(s + 1, n_s), lax.rem(s + n_s - 1, n_s)
    h_next, h_prev = lax.rem(h + 1, n_h), lax.rem(h + n_h - 1, n_h)

    def fwd(i):
        return seq_copy(s_send, s_recv, s_ss, s_rs, i, s_next)

    def bwd(i):
        return seq_copy(t_send, t_recv, t_ss, t_rs, i, s_prev)

    def up(i):
        return head_copy(up_send, up_recv, up_ss, up_rs, i, h_next)

    def down(i):
        return head_copy(dn_send, dn_recv, dn_ss, dn_rs, i, h_prev)

    s_first, s_last = s == 0, s == n_s - 1
    h_first, h_last = h == 0, h == n_h - 1

    barrier = pltpu.get_barrier_semaphore()

    def greet(cond, **to):
        @pl.when(cond)
        def _():
            pl.semaphore_signal(barrier, inc=1, device_id=to, device_id_type=pl.DeviceIdType.MESH)

    greet(jnp.logical_not(s_first), seq=s_prev)
    greet(jnp.logical_not(s_last), seq=s_next)
    greet(jnp.logical_not(h_first), head=h_prev)
    greet(jnp.logical_not(h_last), head=h_next)

    @pl.when(s_first)
    def _():
        s_recv[...] = jnp.zeros_like(s_recv)

    @pl.when(s_last)
    def _():
        t_recv[...] = jnp.zeros_like(t_recv)

    @pl.when(h_first)
    def _():
        up_recv[...] = jnp.zeros_like(up_recv)

    @pl.when(h_last)
    def _():
        dn_recv[...] = jnp.zeros_like(dn_recv)

    def cols(j):
        return pl.ds(pl.multiple_of(j * DH, DH), DH)

    def states(i):
        for r in range(per):
            j = i * per + r
            own_kv[j] = dot(k_ref[:, cols(j)], v_ref[:, cols(j)], 0, 0)
            own_gs[j] = dot(q_ref[:, cols(j)], g_ref[:, cols(j)], 0, 0)

    row = lax.broadcasted_iota(jnp.int32, (toks, toks), 0)
    col = lax.broadcasted_iota(jnp.int32, (toks, toks), 1)
    causal = row >= col

    def apply(i):
        for r in range(per):
            j = i * per + r
            at = cols(j)
            q, k, v, g = q_ref[:, at], k_ref[:, at], v_ref[:, at], g_ref[:, at]
            prefix = up_recv[i, 0, r].astype(F32) + s_recv[j] + dn_recv[i, 0, r].astype(F32)
            suffix = dn_recv[i, 1, r].astype(F32) + t_recv[j] + up_recv[i, 1, r].astype(F32)
            prefix = (prefix * factor).astype(BF16)
            suffix = (suffix * factor).astype(BF16)
            scores = jnp.where(causal, dot(q, k, 1, 1) * factor, 0.0).astype(BF16)
            dscores = jnp.where(causal, dot(g, v, 1, 1) * factor, 0.0).astype(BF16)
            att_ref[:, at] = (dot(scores, v, 1, 0) + dot(q, prefix, 1, 0)).astype(BF16)
            dq_ref[:, at] = (dot(dscores, k, 1, 0) + dot(g, prefix, 1, 1)).astype(BF16)
            dk_ref[:, at] = (dot(dscores, q, 0, 0) + dot(v, suffix, 1, 1)).astype(BF16)
            dv_ref[:, at] = (dot(scores, g, 0, 0) + dot(k, suffix, 1, 0)).astype(BF16)

    states(0)
    pl.semaphore_wait(
        barrier,
        4 - s_first.astype(jnp.int32) - s_last.astype(jnp.int32)
        - h_first.astype(jnp.int32) - h_last.astype(jnp.int32),
    )

    off_c = SEQ_LAG * (n_s - 1)
    off_e = off_c + TOK_LAG * (n_h - 1)

    def valid(i, *more):
        ok = jnp.logical_and(i >= 0, i < chunks)
        for cond in more:
            ok = jnp.logical_and(ok, cond)
        return ok

    def slot(t, carry):
        i = t - SEQ_LAG * s

        @pl.when(valid(i, s > 0))
        def _():
            fwd(i).wait_recv()

        @pl.when(valid(i, s < n_s - 1))
        def _():
            at = pl.ds(i * per, per)
            s_send[at] = s_recv[at] + own_kv[at]
            fwd(i).start()

        b = t - SEQ_LAG * (n_s - 1 - s)

        @pl.when(valid(b, s < n_s - 1))
        def _():
            bwd(b).wait_recv()

        @pl.when(valid(b, s > 0))
        def _():
            at = pl.ds(b * per, per)
            t_send[at] = t_recv[at] + own_gs[at]
            bwd(b).start()

        u = t - off_c - TOK_LAG * h

        @pl.when(valid(u, h > 0))
        def _():
            up(u).wait_recv()

        @pl.when(valid(u, h < n_h - 1))
        def _():
            at = pl.ds(u * per, per)
            up_send[u, 0] = (up_recv[u, 0].astype(F32) + (s_recv[at] + own_kv[at])).astype(zdt)
            up_send[u, 1] = (up_recv[u, 1].astype(F32) + t_recv[at]).astype(zdt)
            up(u).start()

        d = t - off_c - TOK_LAG * (n_h - 1 - h)

        @pl.when(valid(d, h < n_h - 1))
        def _():
            down(d).wait_recv()

        @pl.when(valid(d, h > 0))
        def _():
            at = pl.ds(d * per, per)
            dn_send[d, 1] = (dn_recv[d, 1].astype(F32) + (t_recv[at] + own_gs[at])).astype(zdt)
            dn_send[d, 0] = (dn_recv[d, 0].astype(F32) + s_recv[at]).astype(zdt)
            down(d).start()

        @pl.when(t + 1 < chunks)
        def _():
            states(t + 1)

        e = t - off_e

        @pl.when(valid(e))
        def _():
            apply(e)

        return carry

    lax.fori_loop(0, chunks + off_e, slot, 0)

    def drain(i, carry):
        @pl.when(s < n_s - 1)
        def _():
            fwd(i).wait_send()

        @pl.when(s > 0)
        def _():
            bwd(i).wait_send()

        @pl.when(h < n_h - 1)
        def _():
            up(i).wait_send()

        @pl.when(h > 0)
        def _():
            down(i).wait_send()

        return carry

    lax.fori_loop(0, chunks, drain, 0)


def solution(mesh):
    n_s, n_h = mesh.shape["seq"], mesh.shape["head"]

    def shards(queries, key_rows, value_rows, out_grad):
        toks, width = queries.shape
        heads = width // DH
        per = HEADS_PER_CHUNK
        chunks = heads // per
        factor = float(DH * toks * n_h * n_s) ** (-0.5)
        zdt = BF16 if n_h <= 4 else F32
        state = pltpu.VMEM((heads, DH, DH), F32)
        hop = pltpu.VMEM((chunks, 2, per, DH, DH), zdt)
        vmem = pl.BlockSpec(memory_space=pltpu.VMEM)
        return pl.pallas_call(
            functools.partial(kernel, n_s, n_h, heads, per, factor, zdt),
            out_shape=[jax.ShapeDtypeStruct((toks, width), BF16)] * 4,
            in_specs=[vmem] * 4,
            out_specs=[vmem] * 4,
            scratch_shapes=[state] * 6 + [hop] * 4 + [pltpu.SemaphoreType.DMA((chunks,))] * 8,
            compiler_params=pltpu.CompilerParams(
                collective_id=0, has_side_effects=True, vmem_limit_bytes=48 * 1024 * 1024
            ),
        )(queries, key_rows, value_rows, out_grad)

    placed = (P(("rep", "seq", "head"), None),) * 4
    return jax.shard_map(
        shards, mesh=mesh, in_specs=placed, out_specs=placed, check_vma=False
    )
```

time: 175 us -> 93.2 us (0.53); the launches traced: 172 us -> 92.9 us
  waiting for transfers between devices: 97 us -> 0 us
  Pallas kernels: 0 us -> 84.9 us
  starting transfers between devices: 31.3 us -> 0 us
  between operations: 14.3 us -> 0.65 us
  local copies, waits for them, and re-layouts: 17.1 us -> 7.33 us
  matrix products: 8.13 us -> 0 us
  other arithmetic: 3.83 us -> 0 us
    all_to_all x8 -> x0, waiting for transfers between devices: 87.2 us -> none  [the longest x1 13.9 us: shards(): lax.all_to_all(to_heads(out_grad), 'head', split_axis=1, concat_axis=0, t...]
    pallas_call x0 -> x1, Pallas kernels: none -> 84.9 us  [shards(): pl.pallas_call(functools.partial(kernel, n_s, n_h, heads, per, factor, zd...]
    all_to_all x8 -> x0, starting transfers between devices: 31.2 us -> none  [the longest x1 4.87 us: shards(): lax.all_to_all(to_heads(key_rows), 'head', split_axis=1, concat_axis=0, t...]
    reshape x12 -> x0, local copies, waits for them, and re-layouts: 12.6 us -> none  [the longest x4 4.54 us: per_head(): item.astype(bf16).reshape(seq_rows, 1, heads_here, DH)]
    all_gather x2 -> x0, waiting for transfers between devices: 9.71 us -> none  [the longest x1 9.71 us: per_head(): lax.all_gather(grad_total[None], 'seq', axis=0, tiled=True)]
    dot_general x12 -> x0, matrix products: 8.13 us -> none  [the longest x1 1.48 us: per_head(): jnp.einsum('bhts,bthe->bshe', scores, grad_blocks, preferred_element_type...]
    unnamed x18 -> x12, local copies, waits for them, and re-layouts: 1.9 us -> 7.33 us
    reduce_sum x2 -> x0, other arithmetic: 3.79 us -> none  [the longest x1 1.94 us: per_head(): span_prefix = jnp.sum(pieces[0] * below_me, 0)]
  transfers between devices with their start and end apart: 10 -> 0, of which waited for: 8 -> 0; matrix products, arithmetic and copies ran while one was open for 14% -> 0% of each run, Pallas kernels for 0% -> 0%
where the time goes in v1:
time: 93.2 us; the launch traced here: 92.9 us
  Pallas kernels  84.9 us (91%)
  local copies, waits for them, and re-layouts  7.33 us (8%)
    pallas_call x1, Pallas kernels, shards(): pl.pallas_call(functools.partial(kernel, n_s, n_h, heads, per, factor, zd...  84.9 us
    unnamed x12, local copies, waits for them, and re-layouts  7.33 us

profile of v1, /device:TPU:2, one launch (start us, length us, event | category | flops | bytes accessed | tf_op | source)
XLA Modules:
  0.0 92.9 jit_solution(17016938834702852863)
XLA Ops:
  0.6 0.0 copy-start
  0.6 1.0 %copy-done = bf16[64,4096]{1,0:T(8,128)(2,1)S(1)} copy-done((bf16[64,4096]{1,0:T(8,128)(2,1)S(1)}, bf16[64,4096]{1,0:T(8,128)(2,1)}, u32[]{:S(2)}) %copy-start) | copy-done | bytes 524312
  1.7 0.0 copy-start.1
  1.7 1.0 %copy-done.1 = bf16[64,4096]{1,0:T(8,128)(2,1)S(1)} copy-done((bf16[64,4096]{1,0:T(8,128)(2,1)S(1)}, bf16[64,4096]{1,0:T(8,128)(2,1)}, u32[]{:S(2)}) %copy-start.1) | copy-done | bytes 524312
  2.7 0.0 copy-start.2
  2.7 1.0 %copy-done.2 = bf16[64,4096]{1,0:T(8,128)(2,1)S(1)} copy-done((bf16[64,4096]{1,0:T(8,128)(2,1)S(1)}, bf16[64,4096]{1,0:T(8,128)(2,1)}, u32[]{:S(2)}) %copy-start.2) | copy-done | bytes 524312
  3.8 0.0 copy-start.3
  3.8 1.0 %copy-done.3 = bf16[64,4096]{1,0:T(8,128)(2,1)S(1)} copy-done((bf16[64,4096]{1,0:T(8,128)(2,1)S(1)}, bf16[64,4096]{1,0:T(8,128)(2,1)}, u32[]{:S(2)}) %copy-start.3) | copy-done | bytes 524312
  4.8 84.9 %shard_map.75 = (bf16[64,4096]{1,0:T(8,128)(2,1)S(1)}, bf16[64,4096]{1,0:T(8,128)(2,1)S(1)}, bf16[64,4096]{1,0:T(8,128)(2,1)S(1)}, bf16[64,4096]{1,0:T(8,128)(2,1)S(1)}) custom-call(bf16[64,4096]{1,0:T(8,128)(2,1)S(1)} %copy-done, bf16[64,4096]{1,0:T(8,128)(2,1)S(1)} %copy-done.1, bf16[64,4096]{1,0:T(8,128)(2,1)S(1)} %copy-done.2, bf16[64,4096]{1,0:T(8,128)(2,1)S(1)} %copy-done.3), custom_call_target="tpu_custom_call" | custom-call | tf_op jit(solution)/shard_map/pallas_call | solution.py:247
  89.7 0.8 copy.12
  90.5 0.8 copy.13
  91.3 0.8 copy.14
  92.1 0.8 copy.15
Async XLA Ops:
  0.6 1.0 %copy-start = (bf16[64,4096]{1,0:T(8,128)(2,1)S(1)}, bf16[64,4096]{1,0:T(8,128)(2,1)}, u32[]{:S(2)}) copy-start(bf16[64,4096]{1,0:T(8,128)(2,1)} %q_ref.1) | copy-start | bytes 1572868
  1.7 1.0 %copy-start.1 = (bf16[64,4096]{1,0:T(8,128)(2,1)S(1)}, bf16[64,4096]{1,0:T(8,128)(2,1)}, u32[]{:S(2)}) copy-start(bf16[64,4096]{1,0:T(8,128)(2,1)} %k_ref.1) | copy-start | bytes 1572868
  2.7 1.0 %copy-start.2 = (bf16[64,4096]{1,0:T(8,128)(2,1)S(1)}, bf16[64,4096]{1,0:T(8,128)(2,1)}, u32[]{:S(2)}) copy-start(bf16[64,4096]{1,0:T(8,128)(2,1)} %v_ref.1) | copy-start | bytes 1572868
  3.8 1.0 %copy-start.3 = (bf16[64,4096]{1,0:T(8,128)(2,1)S(1)}, bf16[64,4096]{1,0:T(8,128)(2,1)}, u32[]{:S(2)}) copy-start(bf16[64,4096]{1,0:T(8,128)(2,1)} %g_ref.1) | copy-start | bytes 1572868

commit v2 on v1

v2 whole, which is shorter than its diff:
```python
import functools

import jax
import jax.numpy as jnp
from jax import lax
from jax.experimental import pallas as pl
from jax.experimental.pallas import tpu as pltpu
from jax.sharding import PartitionSpec as P

DH = 128
SPLIT = 1
CORE_LAG = 1
CHIP_LAG = 2
TOK_LAG = 3
GROUP = 8
VMEM = 62 * 1024 * 1024

F32 = jnp.float32
BF16 = jnp.bfloat16
MESH = pl.DeviceIdType.MESH


def dot(a, b, ca, cb):
    return lax.dot_general(a, b, (((ca,), (cb,)), ((), ())), preferred_element_type=F32)


def kernel(
    n_s, n_h, heads, factor, xdt, zdt,
    q_hbm, k_hbm, v_hbm, g_hbm,
    att_hbm, dq_hbm, dk_hbm, dv_hbm,
    q_ref, k_ref, v_ref, g_ref, att_ref, dq_ref, dk_ref, dv_ref,
    own, pair, s_all, t_all, f_send, f_recv, b_send, b_recv,
    up_send, up_recv, dn_send, dn_recv,
    in_sem, out_sem, c_ss, c_rs, f_ss, f_rs, b_ss, b_rs, up_ss, up_rs, dn_ss, dn_rs,
):
    s = lax.axis_index("seq")
    h = lax.axis_index("head")
    n_p = n_s // 2
    p, c = s // 2, lax.rem(s, 2)
    units = heads * SPLIT
    rows = DH // SPLIT
    toks = q_ref.shape[0]
    groups = heads // GROUP

    def fetch(g):
        at = pl.ds(pl.multiple_of(g * GROUP * DH, GROUP * DH), GROUP * DH)
        return [
            pltpu.make_async_copy(src.at[:, at], dst.at[:, at], in_sem.at[n, g])
            for n, (src, dst) in enumerate(
                ((k_hbm, k_ref), (v_hbm, v_ref), (q_hbm, q_ref), (g_hbm, g_ref))
            )
        ]

    def put(g):
        at = pl.ds(pl.multiple_of(g * GROUP * DH, GROUP * DH), GROUP * DH)
        return [
            pltpu.make_async_copy(src.at[:, at], dst.at[:, at], out_sem.at[n, g])
            for n, (src, dst) in enumerate(
                ((att_ref, att_hbm), (dq_ref, dq_hbm), (dk_ref, dk_hbm), (dv_ref, dv_hbm))
            )
        ]

    for g in range(groups):
        for copy in fetch(g):
            copy.start()

    def remote(src, dst, ss, rs, i, to):
        return pltpu.make_async_remote_copy(
            src_ref=src, dst_ref=dst, send_sem=ss.at[i], recv_sem=rs.at[i],
            device_id=to, device_id_type=MESH,
        )

    other = 2 * p + (1 - c)
    s_up, s_dn = lax.rem(s + 2, n_s), lax.rem(s + n_s - 2, n_s)
    h_up, h_dn = lax.rem(h + 1, n_h), lax.rem(h + n_h - 1, n_h)

    def swap(i):
        return remote(own.at[i], pair.at[i], c_ss, c_rs, i, {"seq": other})

    def fwd(i):
        return remote(f_send.at[i], f_recv.at[i], f_ss, f_rs, i, {"seq": s_up})

    def bwd(i):
        return remote(b_send.at[i], b_recv.at[i], b_ss, b_rs, i, {"seq": s_dn})

    def up(i, n):
        return remote(
            up_send.at[i, pl.ds(0, n)], up_recv.at[i, pl.ds(0, n)], up_ss, up_rs, i, {"head": h_up}
        )

    def down(i, n):
        return remote(
            dn_send.at[i, pl.ds(0, n)], dn_recv.at[i, pl.ds(0, n)], dn_ss, dn_rs, i, {"head": h_dn}
        )

    p_first, p_last = p == 0, p == n_p - 1
    s_first, s_last = s == 0, s == n_s - 1
    h_first, h_last = h == 0, h == n_h - 1
    no = jnp.logical_not

    barrier = pltpu.get_barrier_semaphore()

    def greet(**to):
        pl.semaphore_signal(barrier, inc=1, device_id=to, device_id_type=MESH)

    greet(seq=other)
    pl.when(no(p_first))(lambda: greet(seq=s_dn))
    pl.when(no(p_last))(lambda: greet(seq=s_up))
    pl.when(no(h_first))(lambda: greet(head=h_dn))
    pl.when(no(h_last))(lambda: greet(head=h_up))

    @pl.when(p_first)
    def _():
        f_recv[...] = jnp.zeros_like(f_recv)

    @pl.when(p_last)
    def _():
        b_recv[...] = jnp.zeros_like(b_recv)

    @pl.when(h_first)
    def _():
        up_recv[:, 0] = jnp.zeros_like(up_recv[:, 0])

    @pl.when(h_last)
    def _():
        dn_recv[:, 0] = jnp.zeros_like(dn_recv[:, 0])

    @pl.when(jnp.logical_or(h_first, s_last))
    def _():
        up_recv[:, 1] = jnp.zeros_like(up_recv[:, 1])

    @pl.when(jnp.logical_or(h_last, s_first))
    def _():
        dn_recv[:, 1] = jnp.zeros_like(dn_recv[:, 1])

    def cols(j):
        return pl.ds(pl.multiple_of(j * DH, DH), DH)

    def states(j):
        at = cols(j)
        kv = dot(k_ref[:, at], v_ref[:, at], 0, 0)
        gs = dot(q_ref[:, at], g_ref[:, at], 0, 0)
        for r in range(SPLIT):
            own[j * SPLIT + r, 0] = kv[r * rows:(r + 1) * rows]
            own[j * SPLIT + r, 1] = gs[r * rows:(r + 1) * rows]

    row = lax.broadcasted_iota(jnp.int32, (toks, toks), 0)
    col = lax.broadcasted_iota(jnp.int32, (toks, toks), 1)
    causal = row >= col

    def apply(j):
        at = cols(j)
        q, k, v, g = q_ref[:, at], k_ref[:, at], v_ref[:, at], g_ref[:, at]
        part = pl.ds(j * SPLIT, SPLIT)
        prefix = up_recv[part, 0].astype(F32) + s_all[part] + dn_recv[part, 1].astype(F32)
        suffix = dn_recv[part, 0].astype(F32) + t_all[part] + up_recv[part, 1].astype(F32)
        prefix = (prefix * factor).astype(BF16).reshape(DH, DH)
        suffix = (suffix * factor).astype(BF16).reshape(DH, DH)
        scores = jnp.where(causal, dot(q, k, 1, 1) * factor, 0.0).astype(BF16)
        dscores = jnp.where(causal, dot(g, v, 1, 1) * factor, 0.0).astype(BF16)
        att_ref[:, at] = (dot(scores, v, 1, 0) + dot(q, prefix, 1, 0)).astype(BF16)
        dq_ref[:, at] = (dot(dscores, k, 1, 0) + dot(g, prefix, 1, 1)).astype(BF16)
        dk_ref[:, at] = (dot(dscores, q, 0, 0) + dot(v, suffix, 1, 1)).astype(BF16)
        dv_ref[:, at] = (dot(scores, g, 0, 0) + dot(k, suffix, 1, 0)).astype(BF16)

    for copy in fetch(0):
        copy.wait()
    states(0)
    pl.semaphore_wait(
        barrier,
        5 - p_first.astype(jnp.int32) - p_last.astype(jnp.int32)
        - h_first.astype(jnp.int32) - h_last.astype(jnp.int32),
    )
    for r in range(SPLIT):
        swap(r).start()

    off_z = CORE_LAG + CHIP_LAG * (n_p - 1)
    off_e = off_z + TOK_LAG * (n_h - 1)

    def valid(i, *more):
        ok = jnp.logical_and(i >= 0, i < units)
        for cond in more:
            ok = jnp.logical_and(ok, cond)
        return ok

    def slot(t, carry):
        w = t - CORE_LAG

        @pl.when(valid(w))
        def _():
            swap(w).wait_recv()

        f = t - CORE_LAG - CHIP_LAG * p

        @pl.when(valid(f, no(p_first)))
        def _():
            fwd(f).wait_recv()

        @pl.when(valid(f, no(p_last)))
        def _():
            f_send[f] = (f_recv[f].astype(F32) + (own[f, 0] + pair[f, 0])).astype(xdt)
            fwd(f).start()

        b = t - CORE_LAG - CHIP_LAG * (n_p - 1 - p)

        @pl.when(valid(b, no(p_last)))
        def _():
            bwd(b).wait_recv()

        @pl.when(valid(b, no(p_first)))
        def _():
            b_send[b] = (b_recv[b].astype(F32) + (own[b, 1] + pair[b, 1])).astype(xdt)
            bwd(b).start()

        z = t - off_z

        @pl.when(valid(z))
        def _():
            s_all[z] = f_recv[z].astype(F32) + jnp.where(c == 1, pair[z, 0], 0.0)
            t_all[z] = b_recv[z].astype(F32) + jnp.where(c == 0, pair[z, 1], 0.0)

        u = z - TOK_LAG * h

        @pl.when(valid(u, no(h_first), no(s_last)))
        def _():
            up(u, 2).wait_recv()

        @pl.when(valid(u, no(h_first), s_last))
        def _():
            up(u, 1).wait_recv()

        @pl.when(valid(u, no(h_last)))
        def _():
            up_send[u, 0] = (up_recv[u, 0].astype(F32) + (s_all[u] + own[u, 0])).astype(zdt)

            @pl.when(no(s_last))
            def _():
                up_send[u, 1] = (up_recv[u, 1].astype(F32) + t_all[u]).astype(zdt)
                up(u, 2).start()

            @pl.when(s_last)
            def _():
                up(u, 1).start()

        d = z - TOK_LAG * (n_h - 1 - h)

        @pl.when(valid(d, no(h_last), no(s_first)))
        def _():
            down(d, 2).wait_recv()

        @pl.when(valid(d, no(h_last), s_first))
        def _():
            down(d, 1).wait_recv()

        @pl.when(valid(d, no(h_first)))
        def _():
            dn_send[d, 0] = (dn_recv[d, 0].astype(F32) + (t_all[d] + own[d, 1])).astype(zdt)

            @pl.when(no(s_first))
            def _():
                dn_send[d, 1] = (dn_recv[d, 1].astype(F32) + s_all[d]).astype(zdt)
                down(d, 2).start()

            @pl.when(s_first)
            def _():
                down(d, 1).start()

        j = (t + 1) // SPLIT

        @pl.when(jnp.logical_and(lax.rem(t + 1, SPLIT) == 0, j < heads))
        def _():
            @pl.when(lax.rem(j, GROUP) == 0)
            def _():
                for copy in fetch(j // GROUP):
                    copy.wait()

            states(j)
            for r in range(SPLIT):
                swap(j * SPLIT + r).start()

        e = t - off_e

        @pl.when(valid(e, lax.rem(e + 1, SPLIT) == 0))
        def _():
            apply(e // SPLIT)

            @pl.when(lax.rem(e // SPLIT + 1, GROUP) == 0)
            def _():
                for copy in put(e // SPLIT // GROUP):
                    copy.start()

        return carry

    lax.fori_loop(0, units + off_e, slot, 0)

    def drain(i, carry):
        swap(i).wait_send()
        pl.when(no(p_last))(lambda: fwd(i).wait_send())
        pl.when(no(p_first))(lambda: bwd(i).wait_send())
        pl.when(jnp.logical_and(no(h_last), no(s_last)))(lambda: up(i, 2).wait_send())
        pl.when(jnp.logical_and(no(h_last), s_last))(lambda: up(i, 1).wait_send())
        pl.when(jnp.logical_and(no(h_first), no(s_first)))(lambda: down(i, 2).wait_send())
        pl.when(jnp.logical_and(no(h_first), s_first))(lambda: down(i, 1).wait_send())
        return carry

    lax.fori_loop(0, units, drain, 0)
    for g in range(groups):
        for copy in put(g):
            copy.wait()


def solution(mesh):
    n_s, n_h = mesh.shape["seq"], mesh.shape["head"]

    def shards(queries, key_rows, value_rows, out_grad):
        toks, width = queries.shape
        heads = width // DH
        units, rows = heads * SPLIT, DH // SPLIT
        factor = float(DH * toks * n_h * n_s) ** (-0.5)
        xdt = BF16 if n_s <= 4 else F32
        zdt = BF16 if n_h <= 4 else F32
        tokens = pltpu.VMEM((toks, width), BF16)
        both = pltpu.VMEM((units, 2, rows, DH), F32)
        one = pltpu.VMEM((units, rows, DH), F32)
        chip = pltpu.VMEM((units, rows, DH), xdt)
        hop = pltpu.VMEM((units, 2, rows, DH), zdt)
        hbm = pl.BlockSpec(memory_space=pltpu.HBM)
        shape = [jax.ShapeDtypeStruct((toks, width), BF16)] * 4
        dma = pltpu.SemaphoreType.DMA
        return pl.pallas_call(
            functools.partial(kernel, n_s, n_h, heads, factor, xdt, zdt),
            out_shape=shape,
            in_specs=[hbm] * 4,
            out_specs=[hbm] * 4,
            scratch_shapes=[tokens] * 8
            + [both] * 2 + [one] * 2 + [chip] * 4 + [hop] * 4
            + [dma((4, heads // GROUP))] * 2 + [dma((units,))] * 10,
            compiler_params=pltpu.CompilerParams(
                collective_id=0, has_side_effects=True, vmem_limit_bytes=VMEM
            ),
        )(queries, key_rows, value_rows, out_grad)

    placed = (P(("rep", "seq", "head"), None),) * 4
    return jax.shard_map(
        shards, mesh=mesh, in_specs=placed, out_specs=placed, check_vma=False
    )
```

time: 93.2 us -> 70.8 us (0.76)
  Pallas kernels: 84.9 us -> 64.7 us
  local copies, waits for them, and re-layouts: 7.33 us -> 5.18 us
    pallas_call x1, Pallas kernels: 84.9 us -> 64.7 us  [shards(): pl.pallas_call(functools.partial(kernel, n_s, n_h, heads, factor, xdt, zd...]
    unnamed x12 -> x10, local copies, waits for them, and re-layouts: 7.33 us -> 5.18 us
where the time goes in v2:
time: 70.8 us; the launch traced here: 70.5 us
  Pallas kernels  64.7 us (91%)
  local copies, waits for them, and re-layouts  5.18 us (7%)
    pallas_call x1, Pallas kernels, shards(): pl.pallas_call(functools.partial(kernel, n_s, n_h, heads, factor, xdt, zd...  64.7 us
    unnamed x10, local copies, waits for them, and re-layouts  5.18 us

profile of v2, /device:TPU:2, one launch (start us, length us, event | category | flops | bytes accessed | tf_op | source)
XLA Modules:
  0.0 70.5 jit_solution(5371722262397021152)
XLA Ops:
  0.6 64.7 %shard_map.75 = (bf16[64,4096]{1,0:T(8,128)(2,1)}, bf16[64,4096]{1,0:T(8,128)(2,1)}, bf16[64,4096]{1,0:T(8,128)(2,1)}, bf16[64,4096]{1,0:T(8,128)(2,1)}) custom-call(bf16[64,4096]{1,0:T(8,128)(2,1)} %q_hbm.1, bf16[64,4096]{1,0:T(8,128)(2,1)} %k_hbm.1, bf16[64,4096]{1,0:T(8,128)(2,1)} %v_hbm.1, bf16[64,4096]{1,0:T(8,128)(2,1)} %g_hbm.1), custom_call_target="tpu_custom_call" | custom-call | tf_op jit(solution)/shard_map/pallas_call | solution.py:330
  65.3 0.0 copy-start.2
  65.4 1.9 %copy.12 = bf16[64,4096]{1,0:T(8,128)(2,1)} copy(bf16[64,4096]{1,0:T(8,128)(2,1)} %get-tuple-element.8) | data formatting | bytes 1048576
  67.3 0.0 copy-done.2
  67.3 0.0 copy-start.1
  67.3 0.8 %copy.13 = bf16[64,4096]{1,0:T(8,128)(2,1)} copy(bf16[64,4096]{1,0:T(8,128)(2,1)S(1)} %copy-done.2) | data formatting | bytes 1048576
  68.1 0.4 copy-done.1
  68.5 0.0 copy-start
  68.5 0.8 %copy.14 = bf16[64,4096]{1,0:T(8,128)(2,1)} copy(bf16[64,4096]{1,0:T(8,128)(2,1)S(1)} %copy-done.1) | data formatting | bytes 1048576
  69.3 0.4 copy-done
  69.7 0.8 %copy.15 = bf16[64,4096]{1,0:T(8,128)(2,1)} copy(bf16[64,4096]{1,0:T(8,128)(2,1)S(1)} %copy-done) | data formatting | bytes 1048576
Async XLA Ops:
  65.3 1.9 %copy-start.2 = (bf16[64,4096]{1,0:T(8,128)(2,1)S(1)}, bf16[64,4096]{1,0:T(8,128)(2,1)}, u32[]{:S(2)}) copy-start(bf16[64,4096]{1,0:T(8,128)(2,1)} %get-tuple-element.9) | copy-start | bytes 1572868
  67.3 1.2 %copy-start.1 = (bf16[64,4096]{1,0:T(8,128)(2,1)S(1)}, bf16[64,4096]{1,0:T(8,128)(2,1)}, u32[]{:S(2)}) copy-start(bf16[64,4096]{1,0:T(8,128)(2,1)} %get-tuple-element.10) | copy-start | bytes 1572868
  68.5 1.2 %copy-start = (bf16[64,4096]{1,0:T(8,128)(2,1)S(1)}, bf16[64,4096]{1,0:T(8,128)(2,1)}, u32[]{:S(2)}) copy-start(bf16[64,4096]{1,0:T(8,128)(2,1)} %get-tuple-element.11) | copy-start | bytes 1572868

commit v3 on v2

--- a/solution.py
+++ b/solution.py
@@ -13,6 +13,7 @@
 CHIP_LAG = 2
 TOK_LAG = 3
 GROUP = 8
+STEPS = 2
 VMEM = 62 * 1024 * 1024
 
 F32 = jnp.float32
@@ -309,6 +310,11 @@
             copy.wait()
 
 
+def store(*refs):
+    for src, dst in zip(refs[:4], refs[4:]):
+        dst[...] = src[...]
+
+
 def solution(mesh):
     n_s, n_h = mesh.shape["seq"], mesh.shape["head"]
 
@@ -327,7 +333,7 @@
         hbm = pl.BlockSpec(memory_space=pltpu.HBM)
         shape = [jax.ShapeDtypeStruct((toks, width), BF16)] * 4
         dma = pltpu.SemaphoreType.DMA
-        return pl.pallas_call(
+        results = pl.pallas_call(
             functools.partial(kernel, n_s, n_h, heads, factor, xdt, zdt),
             out_shape=shape,
             in_specs=[hbm] * 4,
@@ -340,6 +346,16 @@
             ),
         )(queries, key_rows, value_rows, out_grad)
 
+        block = pl.BlockSpec((toks // STEPS, width), lambda i: (i, 0))
+        return pl.pallas_call(
+            store,
+            grid=(STEPS,),
+            out_shape=shape,
+            in_specs=[block] * 4,
+            out_specs=[block] * 4,
+            compiler_params=pltpu.CompilerParams(vmem_limit_bytes=VMEM),
+        )(*results)
+
     placed = (P(("rep", "seq", "head"), None),) * 4
     return jax.shard_map(
         shards, mesh=mesh, in_specs=placed, out_specs=placed, check_vma=False

time: 70.8 us -> 68.1 us (0.962)
  local copies, waits for them, and re-layouts: 5.18 us -> 0 us
  Pallas kernels: 64.7 us -> 67.3 us
    unnamed x10 -> x0, local copies, waits for them, and re-layouts: 5.18 us -> none
    pallas_call x0 -> x1, Pallas kernels: none -> 2.58 us  [shards(): pl.pallas_call(store, grid=(STEPS,), out_shape=shape, in_specs=[block] *...]
where the time goes in v3:
time: 68.1 us; the launch traced here: 67.9 us
  Pallas kernels  67.3 us (99%)
    pallas_call x1, Pallas kernels, shards(): pl.pallas_call(functools.partial(kernel, n_s, n_h, heads, factor, xdt, zd...  64.7 us
    pallas_call x1, Pallas kernels, shards(): pl.pallas_call(store, grid=(STEPS,), out_shape=shape, in_specs=[block] *...  2.58 us

profile of v3, /device:TPU:2, one launch (start us, length us, event | category | flops | bytes accessed | tf_op | source)
XLA Modules:
  0.0 67.9 jit_solution(9455745517869338209)
XLA Ops:
  0.6 64.7 %shard_map.75 = (bf16[64,4096]{1,0:T(8,128)(2,1)}, bf16[64,4096]{1,0:T(8,128)(2,1)}, bf16[64,4096]{1,0:T(8,128)(2,1)}, bf16[64,4096]{1,0:T(8,128)(2,1)}) custom-call(bf16[64,4096]{1,0:T(8,128)(2,1)} %q_hbm.1, bf16[64,4096]{1,0:T(8,128)(2,1)} %k_hbm.1, bf16[64,4096]{1,0:T(8,128)(2,1)} %v_hbm.1, bf16[64,4096]{1,0:T(8,128)(2,1)} %g_hbm.1), custom_call_target="tpu_custom_call" | custom-call | tf_op jit(solution)/shard_map/pallas_call | solution.py:336
  65.3 2.6 %shard_map.76 = (bf16[64,4096]{1,0:T(8,128)(2,1)}, bf16[64,4096]{1,0:T(8,128)(2,1)}, bf16[64,4096]{1,0:T(8,128)(2,1)}, bf16[64,4096]{1,0:T(8,128)(2,1)}) custom-call(bf16[64,4096]{1,0:T(8,128)(2,1)} %get-tuple-element.8.refs_0_, bf16[64,4096]{1,0:T(8,128)(2,1)} %get-tuple-element.9.refs_1_, bf16[64,4096]{1,0:T(8,128)(2,1)} %get-tuple-element.10.refs_2_, ...), custom_call_target="tpu_custom_call" | custom-call | tf_op jit(solution)/shard_map/pallas_call | solution.py:350

commit v4 on v3

--- a/solution.py
+++ b/solution.py
@@ -166,13 +166,14 @@
 
     for copy in fetch(0):
         copy.wait()
-    states(0)
+    for j in range(GROUP):
+        states(j)
     pl.semaphore_wait(
         barrier,
         5 - p_first.astype(jnp.int32) - p_last.astype(jnp.int32)
         - h_first.astype(jnp.int32) - h_last.astype(jnp.int32),
     )
-    for r in range(SPLIT):
+    for r in range(GROUP * SPLIT):
         swap(r).start()
 
     off_z = CORE_LAG + CHIP_LAG * (n_p - 1)
@@ -184,117 +185,7 @@
             ok = jnp.logical_and(ok, cond)
         return ok
 
-    def slot(t, carry):
-        w = t - CORE_LAG
-
-        @pl.when(valid(w))
-        def _():
-            swap(w).wait_recv()
-
-        f = t - CORE_LAG - CHIP_LAG * p
-
-        @pl.when(valid(f, no(p_first)))
-        def _():
-            fwd(f).wait_recv()
-
-        @pl.when(valid(f, no(p_last)))
-        def _():
-            f_send[f] = (f_recv[f].astype(F32) + (own[f, 0] + pair[f, 0])).astype(xdt)
-            fwd(f).start()
-
-        b = t - CORE_LAG - CHIP_LAG * (n_p - 1 - p)
-
-        @pl.when(valid(b, no(p_last)))
-        def _():
-            bwd(b).wait_recv()
-
-        @pl.when(valid(b, no(p_first)))
-        def _():
-            b_send[b] = (b_recv[b].astype(F32) + (own[b, 1] + pair[b, 1])).astype(xdt)
-            bwd(b).start()
-
-        z = t - off_z
-
-        @pl.when(valid(z))
-        def _():
-            s_all[z] = f_recv[z].astype(F32) + jnp.where(c == 1, pair[z, 0], 0.0)
-            t_all[z] = b_recv[z].astype(F32) + jnp.where(c == 0, pair[z, 1], 0.0)
-
-        u = z - TOK_LAG * h
-
-        @pl.when(valid(u, no(h_first), no(s_last)))
-        def _():
-            up(u, 2).wait_recv()
-
-        @pl.when(valid(u, no(h_first), s_last))
-        def _():
-            up(u, 1).wait_recv()
-
-        @pl.when(valid(u, no(h_last)))
-        def _():
-            up_send[u, 0] = (up_recv[u, 0].astype(F32) + (s_all[u] + own[u, 0])).astype(zdt)
-
-            @pl.when(no(s_last))
-            def _():
-                up_send[u, 1] = (up_recv[u, 1].astype(F32) + t_all[u]).astype(zdt)
-                up(u, 2).start()
-
-            @pl.when(s_last)
-            def _():
-                up(u, 1).start()
-
-        d = z - TOK_LAG * (n_h - 1 - h)
-
-        @pl.when(valid(d, no(h_last), no(s_first)))
-        def _():
-            down(d, 2).wait_recv()
-
-        @pl.when(valid(d, no(h_last), s_first))
-        def _():
-            down(d, 1).wait_recv()
-
-        @pl.when(valid(d, no(h_first)))
-        def _():
-            dn_send[d, 0] = (dn_recv[d, 0].astype(F32) + (t_all[d] + own[d, 1])).astype(zdt)
-
-            @pl.when(no(s_first))
-            def _():
-                dn_send[d, 1] = (dn_recv[d, 1].astype(F32) + s_all[d]).astype(zdt)
-                down(d, 2).start()
-
-            @pl.when(s_first)
-            def _():
-                down(d, 1).start()
-
-        j = (t + 1) // SPLIT
-
-        @pl.when(jnp.logical_and(lax.rem(t + 1, SPLIT) == 0, j < heads))
-        def _():
-            @pl.when(lax.rem(j, GROUP) == 0)
-            def _():
-                for copy in fetch(j // GROUP):
-                    copy.wait()
-
-            states(j)
-            for r in range(SPLIT):
-                swap(j * SPLIT + r).start()
-
-        e = t - off_e
-
-        @pl.when(valid(e, lax.rem(e + 1, SPLIT) == 0))
-        def _():
-            apply(e // SPLIT)
-
-            @pl.when(lax.rem(e // SPLIT + 1, GROUP) == 0)
-            def _():
-                for copy in put(e // SPLIT // GROUP):
-                    copy.start()
-
-        return carry
-
-    lax.fori_loop(0, units + off_e, slot, 0)
-
-    def drain(i, carry):
+    def drain(i):
         swap(i).wait_send()
         pl.when(no(p_last))(lambda: fwd(i).wait_send())
         pl.when(no(p_first))(lambda: bwd(i).wait_send())
@@ -302,9 +193,121 @@
         pl.when(jnp.logical_and(no(h_last), s_last))(lambda: up(i, 1).wait_send())
         pl.when(jnp.logical_and(no(h_first), no(s_first)))(lambda: down(i, 2).wait_send())
         pl.when(jnp.logical_and(no(h_first), s_first))(lambda: down(i, 1).wait_send())
+
+    def slot(t, carry):
+        w = t - CORE_LAG
+
+        @pl.when(valid(w))
+        def _():
+            swap(w).wait_recv()
+
+        f = t - CORE_LAG - CHIP_LAG * p
+
+        @pl.when(valid(f, no(p_first)))
+        def _():
+            fwd(f).wait_recv()
+
+        @pl.when(valid(f, no(p_last)))
+        def _():
+            f_send[f] = (f_recv[f].astype(F32) + (own[f, 0] + pair[f, 0])).astype(xdt)
+            fwd(f).start()
+
+        b = t - CORE_LAG - CHIP_LAG * (n_p - 1 - p)
+
+        @pl.when(valid(b, no(p_last)))
+        def _():
+            bwd(b).wait_recv()
+
+        @pl.when(valid(b, no(p_first)))
+        def _():
+            b_send[b] = (b_recv[b].astype(F32) + (own[b, 1] + pair[b, 1])).astype(xdt)
+            bwd(b).start()
+
+        z = t - off_z
+
+        @pl.when(valid(z))
+        def _():
+            s_all[z] = f_recv[z].astype(F32) + jnp.where(c == 1, pair[z, 0], 0.0)
+            t_all[z] = b_recv[z].astype(F32) + jnp.where(c == 0, pair[z, 1], 0.0)
+
+        u = z - TOK_LAG * h
+
+        @pl.when(valid(u, no(h_first), no(s_last)))
+        def _():
+            up(u, 2).wait_recv()
+
+        @pl.when(valid(u, no(h_first), s_last))
+        def _():
+            up(u, 1).wait_recv()
+
+        @pl.when(valid(u, no(h_last)))
+        def _():
+            up_send[u, 0] = (up_recv[u, 0].astype(F32) + (s_all[u] + own[u, 0])).astype(zdt)
+
+            @pl.when(no(s_last))
+            def _():
+                up_send[u, 1] = (up_recv[u, 1].astype(F32) + t_all[u]).astype(zdt)
+                up(u, 2).start()
+
+            @pl.when(s_last)
+            def _():
+                up(u, 1).start()
+
+        d = z - TOK_LAG * (n_h - 1 - h)
+
+        @pl.when(valid(d, no(h_last), no(s_first)))
+        def _():
+            down(d, 2).wait_recv()
+
+        @pl.when(valid(d, no(h_last), s_first))
+        def _():
+            down(d, 1).wait_recv()
+
+        @pl.when(valid(d, no(h_first)))
+        def _():
+            dn_send[d, 0] = (dn_recv[d, 0].astype(F32) + (t_all[d] + own[d, 1])).astype(zdt)
+
+            @pl.when(no(s_first))
+            def _():
+                dn_send[d, 1] = (dn_recv[d, 1].astype(F32) + s_all[d]).astype(zdt)
+                down(d, 2).start()
+
+            @pl.when(s_first)
+            def _():
+                down(d, 1).start()
+
+        j = (t + 1) // SPLIT + GROUP - 1
+
+        @pl.when(jnp.logical_and(lax.rem(t + 1, SPLIT) == 0, j < heads))
+        def _():
+            @pl.when(lax.rem(j, GROUP) == 0)
+            def _():
+                for copy in fetch(j // GROUP):
+                    copy.wait()
+
+            states(j)
+            for r in range(SPLIT):
+                swap(j * SPLIT + r).start()
+
+        e = t - off_e
+
+        @pl.when(valid(e))
+        def _():
+            drain(e)
+
+        @pl.when(valid(e, lax.rem(e + 1, SPLIT) == 0))
+        def _():
+            apply(e // SPLIT)
+
+            @pl.when(lax.rem(e // SPLIT + 1, GROUP) == 0)
+            def _():
+                for copy in put(e // SPLIT // GROUP):
+                    copy.start()
+
         return carry
 
-    lax.fori_loop(0, units, drain, 0)
+    lax.fori_loop(0, units + off_e, slot, 0)
+
     for g in range(groups):
         for copy in put(g):
             copy.wait()

time: 68.1 us -> 68.5 us (level)
  no operation moved by 1% of the time
where the time goes in v4:
time: 68.5 us; the launch traced here: 68.3 us
  Pallas kernels  67.7 us (99%)
    pallas_call x1, Pallas kernels, shards(): pl.pallas_call(functools.partial(kernel, n_s, n_h, heads, factor, xdt, zd...  65.1 us
    pallas_call x1, Pallas kernels, shards(): pl.pallas_call(store, grid=(STEPS,), out_shape=shape, in_specs=[block] *...  2.58 us

profile of v4, /device:TPU:2, one launch (start us, length us, event | category | flops | bytes accessed | tf_op | source)
XLA Modules:
  0.0 68.3 jit_solution(162590586535760891)
XLA Ops:
  0.6 65.1 %shard_map.75 = (bf16[64,4096]{1,0:T(8,128)(2,1)}, bf16[64,4096]{1,0:T(8,128)(2,1)}, bf16[64,4096]{1,0:T(8,128)(2,1)}, bf16[64,4096]{1,0:T(8,128)(2,1)}) custom-call(bf16[64,4096]{1,0:T(8,128)(2,1)} %q_hbm.1, bf16[64,4096]{1,0:T(8,128)(2,1)} %k_hbm.1, bf16[64,4096]{1,0:T(8,128)(2,1)} %v_hbm.1, bf16[64,4096]{1,0:T(8,128)(2,1)} %g_hbm.1), custom_call_target="tpu_custom_call" | custom-call | tf_op jit(solution)/shard_map/pallas_call | solution.py:339
  65.7 2.6 %shard_map.76 = (bf16[64,4096]{1,0:T(8,128)(2,1)}, bf16[64,4096]{1,0:T(8,128)(2,1)}, bf16[64,4096]{1,0:T(8,128)(2,1)}, bf16[64,4096]{1,0:T(8,128)(2,1)}) custom-call(bf16[64,4096]{1,0:T(8,128)(2,1)} %get-tuple-element.8.refs_0_, bf16[64,4096]{1,0:T(8,128)(2,1)} %get-tuple-element.9.refs_1_, bf16[64,4096]{1,0:T(8,128)(2,1)} %get-tuple-element.10.refs_2_, ...), custom_call_target="tpu_custom_call" | custom-call | tf_op jit(solution)/shard_map/pallas_call | solution.py:353
